TPU v7x, 32 devices: a whole 2x2x4 slice. The times are simulated.
32 devices in a mesh: dp: 8 (over z, y), tensor: 4 (over x, core).
Axes of the slice: x: 2, y: 2, z: 4, core: 2. Of those that a mesh axis runs over, the one named last changes fastest.
Arguments:
- tokens: bfloat16 [16384, 768], P('dp'), may hold values from -6 to 6
- cotangent: bfloat16 [16384, 768], P('dp'), may hold values from -6 to 6
- row_lengths: int32 [32], P('dp'), may hold values from 64 to 512
- present: int32 [32, 64], P('dp'), may hold values 0 or 1
- groups: int32 [32, 512], P('dp'), may hold values from 0 to 63, never falling along the last dimension, each value on 1 to 16 neighbouring positions
- attn_weight: float32 [3, 768, 768], P(None, 'dp', 'tensor'), may hold values from -0.21875 to 0.21875
- attn_first: float32 [3, 768, 768], P(None, 'dp', 'tensor'), may hold values from -24 to 24
- attn_second: float32 [3, 768, 768], P(None, 'dp', 'tensor'), may hold values from 64 to 256
- mix_weight: float32 [768, 768], P('tensor', 'dp'), may hold values from -2.5 to 2.5
- mix_first: float32 [768, 768], P('tensor', 'dp'), may hold values from -32 to 32
- mix_second: float32 [768, 768], P('tensor', 'dp'), may hold values from 128 to 512
- up_weight: float32 [768, 3072], P('dp', 'tensor'), may hold values from -0.21875 to 0.21875
- up_first: float32 [768, 3072], P('dp', 'tensor'), may hold values from -96 to 96
- up_second: float32 [768, 3072], P('dp', 'tensor'), may hold values from 1024 to 4096
- down_weight: float32 [3072, 768], P('tensor', 'dp'), may hold values from -0.109375 to 0.109375
- down_first: float32 [3072, 768], P('tensor', 'dp'), may hold values from -192 to 192
- down_second: float32 [3072, 768], P('tensor', 'dp'), may hold values from 4096 to 16384
- head_bias: float32 [2, 768], P(None, ('tensor', 'dp')), may hold values from -4 to 4
- head_first: float32 [2, 768], P(None, ('tensor', 'dp')), may hold values from -512 to 512
- head_second: float32 [2, 768], P(None, ('tensor', 'dp')), may hold values from 8192 to 32768
- wide_bias: float32 [3072], P(('tensor', 'dp')), may hold values from -4 to 4
- wide_first: float32 [3072], P(('tensor', 'dp')), may hold values from -512 to 512
- wide_second: float32 [3072], P(('tensor', 'dp')), may hold values from 8192 to 32768
- norm_gains: float32 [2, 768], P(None, 'dp'), may hold values from 0.5 to 1.5
- gain_first: float32 [2, 768], P(None, 'dp'), may hold values from -512 to 512
- gain_second: float32 [2, 768], P(None, 'dp'), may hold values from 8192 to 32768
- shift_bias: float32 [4, 768], P(None, 'dp'), may hold values from -4 to 4
- shift_first: float32 [4, 768], P(None, 'dp'), may hold values from -512 to 512
- shift_second: float32 [4, 768], P(None, 'dp'), may hold values from 8192 to 32768
Outputs:
- layer_out: bfloat16 [16384, 768], P('dp')
- tokens_grad: bfloat16 [16384, 768], P('dp')
- attn_weight_new: float32 [3, 768, 768], P(None, 'dp', 'tensor')
- attn_first_new: float32 [3, 768, 768], P(None, 'dp', 'tensor')
- attn_second_new: float32 [3, 768, 768], P(None, 'dp', 'tensor')
- mix_weight_new: float32 [768, 768], P('tensor', 'dp')
- mix_first_new: float32 [768, 768], P('tensor', 'dp')
- mix_second_new: float32 [768, 768], P('tensor', 'dp')
- up_weight_new: float32 [768, 3072], P('dp', 'tensor')
- up_first_new: float32 [768, 3072], P('dp', 'tensor')
- up_second_new: float32 [768, 3072], P('dp', 'tensor')
- down_weight_new: float32 [3072, 768], P('tensor', 'dp')
- down_first_new: float32 [3072, 768], P('tensor', 'dp')
- down_second_new: float32 [3072, 768], P('tensor', 'dp')
- head_bias_new: float32 [2, 768], P(None, ('tensor', 'dp'))
- head_first_new: float32 [2, 768], P(None, ('tensor', 'dp'))
- head_second_new: float32 [2, 768], P(None, ('tensor', 'dp'))
- wide_bias_new: float32 [3072], P(('tensor', 'dp'))
- wide_first_new: float32 [3072], P(('tensor', 'dp'))
- wide_second_new: float32 [3072], P(('tensor', 'dp'))
- norm_gains_new: float32 [2, 768], P(None, 'dp')
- gain_first_new: float32 [2, 768], P(None, 'dp')
- gain_second_new: float32 [2, 768], P(None, 'dp')
- shift_bias_new: float32 [4, 768], P(None, 'dp')
- shift_first_new: float32 [4, 768], P(None, 'dp')
- shift_second_new: float32 [4, 768], P(None, 'dp')
- norm_pairs: float32 [2, 15], replicated
Inputs may be any that keep to these rules, and one draw needn't show every extreme that they name: Along a row the group ids never fall; every one of the 64 groups holds 1 to 16 slots.
All inputs are finite; a program needn't handle non-finite values. No bound on the sum of `present` on one device may be relied on, other than what follows from the above.
Results may differ from a plain program's by a relative error of at most 0.023.
Values may be sent and summed in bfloat16 or wider, within the bound.
No kernel may reach another device: no remote copies, remote signals or barrier semaphores. Data moves between devices by JAX's collectives and lax.ppermute only.
A program may use at most 128 MiB of HBM per device.

v0:
```python
from functools import partial
import jax
import jax.numpy as jnp
from jax import lax
from jax.sharding import PartitionSpec as P

HEAD = 64


def layer_norm(summed):
    center = summed - jnp.mean(summed, axis=-1, keepdims=True)
    spread = jnp.mean(center * center, axis=-1, keepdims=True)
    scaled = lax.rsqrt(spread + 1e-05)
    return (center * scaled, scaled)


def norm_back(upstream, normal, scaled):
    inner_sum = (
        upstream
        - jnp.mean(upstream, axis=-1, keepdims=True)
        - normal * jnp.mean(upstream * normal, axis=-1, keepdims=True)
    )
    return scaled * inner_sum


def visibility(length, present_row, group_row):
    positions = jnp.arange(group_row.shape[0])
    feature_ids = jnp.arange(present_row.shape[0])
    present_key = jnp.sum(
        (group_row[:, None] == feature_ids[None, :]) * present_row[None, :], axis=1
    )
    key_open = (positions < length) & (present_key == 1)
    return key_open[None, :] | (group_row[:, None] == group_row[None, :])


def row_scores(queries, key_rows, visible):
    scale = queries.shape[-1] ** (-0.5)
    scores = (
        jnp.einsum("qhd,khd->hqk", queries, key_rows, preferred_element_type=jnp.float32) * scale
    )
    return jnp.where(visible[None], scores, -1e30)


def row_forward(row_item):
    queries, key_rows, value_rows, visible = row_item
    scores = row_scores(queries, key_rows, visible)
    largest = jnp.max(scores, axis=-1, keepdims=True)
    exponent = jnp.exp(scores - largest)
    row_total = jnp.sum(exponent, axis=-1, keepdims=True)
    probs_low = (exponent / row_total).astype(jnp.bfloat16)
    context = jnp.einsum("hqk,khd->qhd", probs_low, value_rows, preferred_element_type=jnp.float32)
    return (context.astype(jnp.bfloat16), largest + jnp.log(row_total))


def row_backward(row_item):
    queries, key_rows, value_rows, visible, log_total, context_grad = row_item
    scale = queries.shape[-1] ** (-0.5)
    scores = row_scores(queries, key_rows, visible)
    softmax_probs = jnp.exp(scores - log_total)
    probs_low = softmax_probs.astype(jnp.bfloat16)
    value_grad = jnp.einsum(
        "hqk,qhd->khd", probs_low, context_grad, preferred_element_type=jnp.float32
    )
    probs_grad = jnp.einsum(
        "qhd,khd->hqk", context_grad, value_rows, preferred_element_type=jnp.float32
    )
    inner_sum = jnp.sum(softmax_probs * probs_grad, axis=-1, keepdims=True)
    scores_grad = (softmax_probs * (probs_grad - inner_sum)).astype(jnp.bfloat16)
    query_grad = (
        jnp.einsum("hqk,khd->qhd", scores_grad, key_rows, preferred_element_type=jnp.float32)
        * scale
    )
    key_grad = (
        jnp.einsum("hqk,qhd->khd", scores_grad, queries, preferred_element_type=jnp.float32) * scale
    )
    return (
        query_grad.astype(jnp.bfloat16),
        key_grad.astype(jnp.bfloat16),
        value_grad.astype(jnp.bfloat16),
    )


def square_sums(array, piece_count, weight_factor):
    if piece_count == 1:
        return [jnp.sum(array * array) * weight_factor]
    return [jnp.sum(array[member] * array[member]) * weight_factor for member in range(piece_count)]


def trust_factor(trust, offset, piece_count, rank_count):
    if piece_count == 1:
        return trust[offset]
    return trust[offset : offset + piece_count].reshape((piece_count,) + (1,) * (rank_count - 1))


def on_device(
    tokens,
    cotangent,
    row_lengths,
    present,
    groups,
    attn_weight,
    attn_first,
    attn_second,
    mix_weight,
    mix_first,
    mix_second,
    up_weight,
    up_first,
    up_second,
    down_weight,
    down_first,
    down_second,
    head_bias,
    head_first,
    head_second,
    wide_bias,
    wide_first,
    wide_second,
    norm_gains,
    gain_first,
    gain_second,
    shift_bias,
    shift_first,
    shift_second,
):
    bfloat = jnp.bfloat16
    single = jnp.float32
    attn_low, mix_low, up_low, down_low, head_low, wide_low, gain_low, shift_low = (
        lax.all_gather(attn_weight.astype(bfloat), "dp", axis=1, tiled=True),
        lax.all_gather(mix_weight.astype(bfloat), "dp", axis=1, tiled=True),
        lax.all_gather(up_weight.astype(bfloat), "dp", axis=0, tiled=True),
        lax.all_gather(down_weight.astype(bfloat), "dp", axis=1, tiled=True),
        lax.all_gather(head_bias.astype(bfloat), "dp", axis=1, tiled=True),
        lax.all_gather(wide_bias.astype(bfloat), "dp", axis=0, tiled=True),
        lax.all_gather(norm_gains.astype(bfloat), "dp", axis=1, tiled=True),
        lax.all_gather(shift_bias.astype(bfloat), "dp", axis=1, tiled=True),
    )
    gain_float = gain_low.astype(single)
    shift_float = shift_low.astype(single)
    row_count = row_lengths.shape[0]
    row_slots = groups.shape[1]
    local_width = attn_low.shape[2]
    row_shape = (row_count, row_slots, local_width // HEAD, HEAD)
    projected = jnp.einsum("td,kdc->ktc", tokens, attn_low, preferred_element_type=single)
    queries = (projected[0] + head_low[0].astype(single)).astype(bfloat).reshape(row_shape)
    key_rows = projected[1].astype(bfloat).reshape(row_shape)
    value_rows = (projected[2] + head_low[1].astype(single)).astype(bfloat).reshape(row_shape)
    visible = jax.vmap(visibility)(row_lengths, present, groups)
    context, log_total = lax.map(row_forward, (queries, key_rows, value_rows, visible))
    context = context.reshape(row_count * row_slots, local_width)
    attn_part = jnp.dot(context, mix_low, preferred_element_type=single)
    attended = (
        lax.psum(attn_part.astype(jnp.bfloat16), "tensor").astype(jnp.float32) + shift_float[0]
    )
    normal_one, scaled_one = layer_norm(tokens.astype(single) + attended)
    normed = normal_one * gain_float[0] + shift_float[1]
    normed_low = normed.astype(bfloat)
    hidden = jnp.dot(normed_low, up_low, preferred_element_type=single) + wide_low.astype(single)
    active, gelu_back = jax.vjp(partial(jax.nn.gelu, approximate=False), hidden)
    active_low = active.astype(bfloat)
    ffn_part = jnp.dot(active_low, down_low, preferred_element_type=single)
    summed_two = (
        normed
        + lax.psum(ffn_part.astype(jnp.bfloat16), "tensor").astype(jnp.float32)
        + shift_float[2]
    )
    normal_two, scaled_two = layer_norm(summed_two)
    layer_out = (normal_two * gain_float[1] + shift_float[3]).astype(bfloat)
    upstream = cotangent.astype(single)
    gain_two_grad = jnp.sum(upstream * normal_two, axis=0)
    shift_three_grad = jnp.sum(upstream, axis=0)
    back_two = norm_back(upstream * gain_float[1], normal_two, scaled_two)
    shift_two_grad = jnp.sum(back_two, axis=0)
    back_two_low = back_two.astype(bfloat)
    down_grad = jnp.einsum("tf,td->fd", active_low, back_two_low, preferred_element_type=single)
    active_grad = jnp.einsum("td,fd->tf", back_two_low, down_low, preferred_element_type=single)
    hidden_grad = gelu_back(active_grad)[0].astype(bfloat)
    wide_grad = jnp.sum(hidden_grad.astype(single), axis=0)
    up_grad = jnp.einsum("td,tf->df", normed_low, hidden_grad, preferred_element_type=single)
    normed_part = jnp.einsum("tf,df->td", hidden_grad, up_low, preferred_element_type=single)
    normed_grad = back_two + lax.psum(normed_part.astype(jnp.bfloat16), "tensor").astype(
        jnp.float32
    )
    gain_one_grad = jnp.sum(normed_grad * normal_one, axis=0)
    shift_one_grad = jnp.sum(normed_grad, axis=0)
    back_one = norm_back(normed_grad * gain_float[0], normal_one, scaled_one)
    shift_zero_grad = jnp.sum(back_one, axis=0)
    back_one_low = back_one.astype(bfloat)
    mix_grad = jnp.einsum("tc,td->cd", context, back_one_low, preferred_element_type=single)
    context_grad = jnp.einsum(
        "td,cd->tc", back_one_low, mix_low, preferred_element_type=single
    ).astype(bfloat)
    query_grad, key_grad, value_grad = lax.map(
        row_backward,
        (queries, key_rows, value_rows, visible, log_total, context_grad.reshape(row_shape)),
    )
    token_count = row_count * row_slots
    stacked = jnp.stack(
        [
            query_grad.reshape(token_count, local_width),
            key_grad.reshape(token_count, local_width),
            value_grad.reshape(token_count, local_width),
        ]
    )
    head_grad = jnp.stack(
        [jnp.sum(stacked[0].astype(single), axis=0), jnp.sum(stacked[2].astype(single), axis=0)]
    )
    attn_grad = jnp.einsum("td,ktc->kdc", tokens, stacked, preferred_element_type=single)
    token_part = jnp.einsum("ktc,kdc->td", stacked, attn_low, preferred_element_type=single)
    tokens_grad = (
        back_one + lax.psum(token_part.astype(jnp.bfloat16), "tensor").astype(jnp.float32)
    ).astype(bfloat)
    gain_grad = jnp.stack([gain_one_grad, gain_two_grad])
    shift_grad = jnp.stack([shift_zero_grad, shift_one_grad, shift_two_grad, shift_three_grad])
    attn_sum_grad, mix_sum, up_sum, down_sum, head_sum, wide_sum, gain_sum, shift_sum = (
        lax.psum_scatter(attn_grad, "dp", scatter_dimension=1, tiled=True),
        lax.psum_scatter(mix_grad, "dp", scatter_dimension=1, tiled=True),
        lax.psum_scatter(up_grad, "dp", scatter_dimension=0, tiled=True),
        lax.psum_scatter(down_grad, "dp", scatter_dimension=1, tiled=True),
        lax.psum_scatter(head_grad, "dp", scatter_dimension=1, tiled=True),
        lax.psum_scatter(wide_grad, "dp", scatter_dimension=0, tiled=True),
        lax.psum_scatter(gain_grad, "dp", scatter_dimension=1, tiled=True),
        lax.psum_scatter(shift_grad, "dp", scatter_dimension=1, tiled=True),
    )
    masters = (
        attn_weight,
        mix_weight,
        up_weight,
        down_weight,
        head_bias,
        wide_bias,
        norm_gains,
        shift_bias,
    )
    firsts = (
        attn_first,
        mix_first,
        up_first,
        down_first,
        head_first,
        wide_first,
        gain_first,
        shift_first,
    )
    seconds = (
        attn_second,
        mix_second,
        up_second,
        down_second,
        head_second,
        wide_second,
        gain_second,
        shift_second,
    )
    reduced = (attn_sum_grad, mix_sum, up_sum, down_sum, head_sum, wide_sum, gain_sum, shift_sum)
    piece_counts = (3, 1, 1, 1, 2, 1, 2, 4)
    share = 1.0 / lax.axis_size("tensor")
    weight_factors = (1.0, 1.0, 1.0, 1.0, 1.0, 1.0, share, share)
    new_firsts, new_seconds, updates, weight_sq, update_sq = ([], [], [], [], [])
    for master, first_old, second_old, gradient, piece_count, weight_factor in zip(
        masters, firsts, seconds, reduced, piece_counts, weight_factors
    ):
        first_new = 0.5 * first_old + 0.5 * gradient
        second_new = 0.5 * second_old + 0.5 * gradient * gradient
        update = first_new / (jnp.sqrt(second_new) + 1e-06) + 0.01 * master
        new_firsts.append(first_new)
        new_seconds.append(second_new)
        updates.append(update)
        weight_sq.extend(square_sums(master, piece_count, weight_factor))
        update_sq.extend(square_sums(update, piece_count, weight_factor))
    square_totals = lax.psum(
        jnp.stack([jnp.stack(weight_sq), jnp.stack(update_sq)]), ("dp", "tensor")
    )
    norm_pairs = jnp.sqrt(square_totals)
    trust = norm_pairs[0] / (norm_pairs[1] + 1e-06)
    new_masters = []
    offset = 0
    for master, update, piece_count in zip(masters, updates, piece_counts):
        factor = trust_factor(trust, offset, piece_count, master.ndim)
        new_masters.append(master - 0.5 * factor * update)
        offset = offset + piece_count
    return (
        layer_out,
        tokens_grad,
        new_masters[0],
        new_firsts[0],
        new_seconds[0],
        new_masters[1],
        new_firsts[1],
        new_seconds[1],
        new_masters[2],
        new_firsts[2],
        new_seconds[2],
        new_masters[3],
        new_firsts[3],
        new_seconds[3],
        new_masters[4],
        new_firsts[4],
        new_seconds[4],
        new_masters[5],
        new_firsts[5],
        new_seconds[5],
        new_masters[6],
        new_firsts[6],
        new_seconds[6],
        new_masters[7],
        new_firsts[7],
        new_seconds[7],
        norm_pairs,
    )


def solution(mesh):
    return jax.shard_map(
        on_device,
        mesh=mesh,
        in_specs=(
            P("dp", None),
            P("dp", None),
            P("dp"),
            P("dp", None),
            P("dp", None),
            P(None, "dp", "tensor"),
            P(None, "dp", "tensor"),
            P(None, "dp", "tensor"),
            P("tensor", "dp"),
            P("tensor", "dp"),
            P("tensor", "dp"),
            P("dp", "tensor"),
            P("dp", "tensor"),
            P("dp", "tensor"),
            P("tensor", "dp"),
            P("tensor", "dp"),
            P("tensor", "dp"),
            P(None, ("tensor", "dp")),
            P(None, ("tensor", "dp")),
            P(None, ("tensor", "dp")),
            P(("tensor", "dp")),
            P(("tensor", "dp")),
            P(("tensor", "dp")),
            P(None, "dp"),
            P(None, "dp"),
            P(None, "dp"),
            P(None, "dp"),
            P(None, "dp"),
            P(None, "dp"),
        ),
        out_specs=(
            P("dp", None),
            P("dp", None),
            P(None, "dp", "tensor"),
            P(None, "dp", "tensor"),
            P(None, "dp", "tensor"),
            P("tensor", "dp"),
            P("tensor", "dp"),
            P("tensor", "dp"),
            P("dp", "tensor"),
            P("dp", "tensor"),
            P("dp", "tensor"),
            P("tensor", "dp"),
            P("tensor", "dp"),
            P("tensor", "dp"),
            P(None, ("tensor", "dp")),
            P(None, ("tensor", "dp")),
            P(None, ("tensor", "dp")),
            P(("tensor", "dp")),
            P(("tensor", "dp")),
            P(("tensor", "dp")),
            P(None, "dp"),
            P(None, "dp"),
            P(None, "dp"),
            P(None, "dp"),
            P(None, "dp"),
            P(None, "dp"),
            P(),
        ),
        check_vma=False,
    )
```

profile of v0, /device:TPU:0, one launch (start us, length us, event | category | flops | bytes accessed | tf_op | source)
XLA Modules:
  0.0 908.2 jit_solution(8584713637614694734)
XLA Ops:
  9.2 38.6 %all_gather.24 = bf16[3,768,192]{2,0,1:T(4,128)(2,1)S(1)} all-gather(bf16[3,96,192]{2,0,1:T(4,128)(2,1)S(1)} %copy.160), channel_id=1, replica_groups=mesh['dp'=8,'tensor'=4] {'dp'}, dimensions={1}, use_global_device_ids=true | all-gather | bytes 995328 | tf_op jit(solution)/shard_map/all_gather | solution.py:129
  47.8 5.2 convolution_bitcast_fusion
  58.8 18.9 %all-gather = bf16[8,24,2]{1,2,0:T(2,128)(2,1)S(1)} all-gather(bf16[1,24,2]{1,2,0:T(2,128)(2,1)S(1)} %convert_bitcast_fusion.2), channel_id=1, replica_groups=mesh['dp'=8,'tensor'=4] {'dp'}, dimensions={0}, use_global_device_ids=true | all-gather | bytes 864 | tf_op jit(solution)/shard_map/all_gather | solution.py:133
  81.6 2.9 fusion.72
  85.5 15.5 %while.26 = (s32[]{:T(128)}, bf16[4,512,3,64]{1,3,2,0:T(8,128)(2,1)}, f32[4,3,512,1]{2,1,3,0:T(4,128)}, bf16[4,512,3,64]{1,3,2,0:T(8,128)(2,1)S(1)}, pred[4,512,...) while((s32[]{:T(128)}, ...), condition=%wide.region_4.5_spmd, body=%wide.region_1.4_spmd.sunk | while | flops 210860544 | bytes 11592281 | solution.py:149
  108.4 31.2 %all_gather.26 = bf16[192,768]{0,1:T(8,128)(2,1)S(1)} all-gather(bf16[192,96]{0,1:T(8,128)(2,1)} %copy.167), channel_id=1, replica_groups=mesh['dp'=8,'tensor'=4] {'dp'}, dimensions={1}, use_global_device_ids=true | all-gather | bytes 331776 | tf_op jit(solution)/shard_map/all_gather | solution.py:130
  139.6 3.9 convolution_convert_fusion.2
  147.0 16.5 %all-gather.1 = bf16[8,96,4]{1,2,0:T(4,128)(2,1)S(1)} all-gather(bf16[1,96,4]{1,2,0:T(4,128)(2,1)S(1)} %convert_bitcast_fusion), channel_id=1, replica_groups=mesh['dp'=8,'tensor'=4] {'dp'}, dimensions={0}, use_global_device_ids=true | all-gather | bytes 6912 | tf_op jit(solution)/shard_map/all_gather | solution.py:136
  166.4 18.0 %all-gather.2 = bf16[8,96,2]{1,2,0:T(2,128)(2,1)S(1)} all-gather(bf16[1,96,2]{1,2,0:T(2,128)(2,1)S(1)} %convert_bitcast_fusion.1), channel_id=1, replica_groups=mesh['dp'=8,'tensor'=4] {'dp'}, dimensions={0}, use_global_device_ids=true | all-gather | bytes 3456 | tf_op jit(solution)/shard_map/all_gather | solution.py:135
  189.9 17.7 %all-reduce = bf16[768]{0:T(1024)(128)(2,1)S(1)} all-reduce(bf16[768]{0:T(1024)(128)(2,1)S(1)} %dynamic-update-slice), channel_id=1, replica_groups=mesh['dp'=8,'tensor'=4] {'dp'}, use_global_device_ids=true, to_apply=%add | all-reduce | flops 768 | bytes 3072
  209.3 3.1 fusion.68
  214.9 20.6 %multiply_convert_fusion.1 = (bf16[2048,768]{1,0:T(8,128)(2,1)}, f32[2048,768]{1,0:T(8,128)}, f32[2048,768]{1,0:T(8,128)}) fusion(f32[768]{0:T(1024)} %convert_element_type.165, bf16[768,768]{1,0:T(8,128)(2,1)} %all-gather.6.cloned.1.call-done, f32[768]{0:T(1024)} %get-tuple-element.367, f32[768]{0:T(1024)S(1)} %get-tuple-element.370, ...), kind=kOutput, calls=%fused_computation.83 | convolution fusion | flops 2533883904 | bytes 23228416 | tf_op jit(solution)/shard_map/dot_general | solution.py:158
  235.4 6.5 convolution_convert_fusion.1
  242.3 68.4 %all-reduce.11.cloned.1.call-done = bf16[2048,768]{1,0:T(8,128)(2,1)} async-done(((bf16[2048,768]{1,0:T(8,128)(2,1)}), bf16[2048,768]{1,0:T(8,128)(2,1)}) %all-reduce.11.cloned.1.call-update) | async-done | bytes 3145744 | tf_op jit(solution)/shard_map/psum | solution.py:164
  310.7 4.8 fusion.119
  317.4 3.6 fusion.61
  321.1 3.8 fusion.58
  324.9 9.4 %convert_reduce_fusion.1 = (f32[768]{0:T(1024)}, bf16[2048,768]{1,0:T(8,128)(2,1)S(1)}) fusion(f32[2048,768]{1,0:T(8,128)S(1)} %bitcast.250, bf16[768,768]{0,1:T(8,128)(2,1)S(1)} %copy-done.57, f32[2048,768]{1,0:T(8,128)S(1)} %get-tuple-element.457, f32[2048,768]{1,0:T(8,128)} %get-tuple-element.471, f32[768]{0:T(1024)S(1)} %copy-done.43), kind=kOutput, calls=%fused_computation.74 | convolution fusion | flops 2444229888 | bytes 23205888 | tf_op jit(solution)/shard_map/td,fd->tf/dot_general | solution.py:176
  335.9 4.0 convolution_convert_fusion
  342.6 66.1 %all-reduce.13.cloned.1.call-done = bf16[2048,768]{1,0:T(8,128)(2,1)} async-done(((bf16[2048,768]{1,0:T(8,128)(2,1)}), bf16[2048,768]{1,0:T(8,128)(2,1)}) %all-reduce.13.cloned.1.call-update) | async-done | bytes 3145744 | tf_op jit(solution)/shard_map/psum | solution.py:181
  408.7 7.3 multiply_reduce_fusion.1
  416.0 8.1 fusion.111
  431.7 5.3 fusion.86
  437.1 7.7 fusion.91
  444.8 7.9 fusion.77
  452.8 4.9 convolution_convert_fusion.3
  457.7 3.1 reshape.246
  465.9 51.0 %while.27 = (s32[]{:T(128)}, bf16[4,512,3,64]{1,3,2,0:T(8,128)(2,1)}, bf16[4,512,3,64]{1,3,2,0:T(8,128)(2,1)}, bf16[4,512,3,64]{1,3,2,0:T(8,128)(2,1)}, bf16[4,5...) while((s32[]{:T(128)}, ...), condition=%wide.region_18.19_spmd, body=%wide.region_16.18_spmd.sunk | while | flops 510884352 | bytes 26381428 | solution.py:193
  516.9 2.6 copy.172
  519.6 2.8 stack_reshape.9
  522.4 2.6 copy.173
  525.0 2.8 stack_reshape.10
  527.8 2.7 copy.174
  530.5 2.8 stack_reshape.11
  538.3 3.2 fusion.83
  541.5 3.2 copy.187
  544.7 2.8 reshape.264
  560.5 21.7 %all-reduce.3 = (f32[2,192]{1,0:T(2,128)S(1)}, f32[768]{0:T(1024)S(1)}) all-reduce(f32[2,192]{1,0:T(2,128)S(1)} %pad_maximum_fusion.2, f32[768]{0:T(1024)S(1)} %copy-done.42), channel_id=6, replica_groups=mesh['dp'=8,'tensor'=4] {'dp'}, use_global_device_ids=true, to_apply=%region_47.48.clone | all-reduce | flops 1152 | bytes 9216
  583.6 6.7 bitcast_convert_fusion
  599.7 19.1 %reduce-scatter.22.cloned.1.call-done = f32[96,192]{1,0:T(8,128)} async-done(((f32[768,192]{1,0:T(8,128)}), f32[96,192]{1,0:T(8,128)}) %reduce-scatter.22.cloned.1.call-update) | async-done | bytes 73744
  621.2 69.8 %reduce-scatter.16.cloned.1.call-done = f32[96,768]{1,0:T(8,128)} async-done(((f32[768,768]{1,0:T(8,128)}), f32[96,768]{1,0:T(8,128)}) %reduce-scatter.16.cloned.1.call-update) | async-done | bytes 294928 | tf_op jit(solution)/shard_map/reduce_scatter | solution.py:218
  692.8 70.3 %reduce-scatter.18.cloned.1.call-done = f32[768,96]{0,1:T(8,128)} async-done(((f32[768,768]{0,1:T(8,128)}), f32[768,96]{0,1:T(8,128)}) %reduce-scatter.18.cloned.1.call-update) | async-done | bytes 294928 | tf_op jit(solution)/shard_map/reduce_scatter | solution.py:219
  763.1 2.7 multiply_reduce_fusion.8
  765.8 6.3 stack.157
  772.0 60.6 %reduce-scatter.20.cloned.1.call-done = f32[96,576]{1,0:T(8,128)} async-done(((f32[768,576]{1,0:T(8,128)}), f32[96,576]{1,0:T(8,128)}) %reduce-scatter.20.cloned.1.call-update) | async-done | bytes 221200
  836.5 5.9 stack.185
  843.2 6.1 add_convert_fusion
  849.3 39.4 %psum.39 = f32[2,15]{1,0:T(2,128)S(1)} all-reduce(f32[2,15]{1,0:T(2,128)S(1)} %pad_maximum_fusion.3), channel_id=1, replica_groups=mesh['dp'=8,'tensor'=4] {'dp','tensor'}, use_global_device_ids=true, to_apply=%region_67.68 | all-reduce | flops 30 | bytes 240 | tf_op jit(solution)/shard_map/psum | solution.py:271
  (315 shorter events, 157.9 us)
Async XLA Ops:
  8.0 201.3 %all-reduce.9.cloned.1.call-start = ((), (), s32[]{:S(2)}) async-start(), calls=%async_computation.6 | async-start | bytes 6291456 | tf_op jit(solution)/shard_map/psum | solution.py:153
  53.4 27.1 %copy-start.29 = (s32[4,512]{1,0:T(4,128)S(1)}, s32[4,512]{1,0:T(4,128)}, u32[]{:S(2)}) copy-start(s32[4,512]{1,0:T(4,128)} %param.37) | copy-start | bytes 24580
  53.4 27.1 %copy-start.44 = (s32[4,64]{1,0:T(4,128)S(1)}, s32[4,64]{1,0:T(4,128)}, u32[]{:S(2)}) copy-start(s32[4,64]{1,0:T(4,128)} %param.36) | copy-start | bytes 3076
  53.4 27.2 %copy-start.55 = (s32[4]{0:T(128)S(1)}, s32[4]{0:T(128)}, u32[]{:S(2)}) copy-start(s32[4]{0:T(128)} %param.35) | copy-start | bytes 52
  85.5 22.2 %copy-start.18 = (f32[192,96]{1,0:T(8,128)S(1)}, f32[192,96]{1,0:T(8,128)}, u32[]{:S(2)}) copy-start(f32[192,96]{1,0:T(8,128)} %param.41) | copy-start | bytes 221188
  104.7 42.3 %copy-start.31 = (f32[4,96]{1,0:T(4,128)S(1)}, f32[4,96]{1,0:T(4,128)}, u32[]{:S(2)}) copy-start(f32[4,96]{1,0:T(4,128)} %param.59) | copy-start | bytes 4612
  104.7 104.7 %copy-start = (bf16[2048,768]{1,0:T(8,128)(2,1)S(1)}, bf16[2048,768]{1,0:T(8,128)(2,1)}, u32[]{:S(2)}) copy-start(bf16[2048,768]{1,0:T(8,128)(2,1)} %param.33) | copy-start | bytes 9437188
  143.4 71.4 %all-gather.6.cloned.1.call-start = ((), (), s32[]{:S(2)}) async-start(), calls=%async_computation.7 | async-start | bytes 1327104 | tf_op jit(solution)/shard_map/all_gather | solution.py:131
  145.2 90.3 %all-gather.8.cloned.1.call-start = ((), (), s32[]{:S(2)}) async-start(), calls=%async_computation.8 | async-start | bytes 1327104 | tf_op jit(solution)/shard_map/all_gather | solution.py:132
  146.9 163.8 %all-reduce.11.cloned.1.call-start = ((), (), s32[]{:S(2)}) async-start(), calls=%async_computation.9 | async-start | bytes 6291456 | tf_op jit(solution)/shard_map/psum | solution.py:164
  242.0 166.7 %all-reduce.13.cloned.1.call-start = ((), (), s32[]{:S(2)}) async-start(), calls=%async_computation.10 | async-start | bytes 6291456 | tf_op jit(solution)/shard_map/psum | solution.py:181
  317.4 7.5 slice-start
  324.9 9.4 %copy-start.3 = (f32[2048,768]{1,0:T(8,128)}, f32[2048,768]{1,0:T(8,128)S(1)}, u32[]{:S(2)}) copy-start(f32[2048,768]{1,0:T(8,128)S(1)} %get-tuple-element.457) | copy-start | bytes 18874372
  324.9 11.1 %copy-start.56 = (bf16[768,768]{1,0:T(8,128)(2,1)S(1)}, bf16[768,768]{1,0:T(8,128)(2,1)}, u32[]{:S(2)}) copy-start(bf16[768,768]{1,0:T(8,128)(2,1)} %all-gather.6.cloned.1.call-done) | copy-start | bytes 3538948
  340.0 251.7 %reduce-scatter.24.cloned.1.call-start = ((), (), s32[]{:S(2)}) async-start(), calls=%async_computation.16 | async-start | bytes 442368
  416.0 9.9 %copy-start.34 = (f32[1,768]{1,0:T(1,128)S(1)}, f32[1,768]{1,0:T(1,128)}, u32[]{:S(2)}) copy-start(f32[1,768]{1,0:T(1,128)} %stack.172) | copy-start | bytes 9220
  428.1 166.9 %reduce-scatter.26.cloned.1.call-start = ((), (), s32[]{:S(2)}) async-start(), calls=%async_computation.17 | async-start | bytes 442368
  431.2 187.7 %reduce-scatter.22.cloned.1.call-start = ((), (), s32[]{:S(2)}) async-start(), calls=%async_computation.15 | async-start | bytes 884736
  437.0 254.0 %reduce-scatter.16.cloned.1.call-start = ((), (), s32[]{:S(2)}) async-start(), calls=%async_computation.12 | async-start | bytes 2654208 | tf_op jit(solution)/shard_map/reduce_scatter | solution.py:218
  444.8 318.3 %reduce-scatter.18.cloned.1.call-start = ((), (), s32[]{:S(2)}) async-start(), calls=%async_computation.13 | async-start | bytes 2654208 | tf_op jit(solution)/shard_map/reduce_scatter | solution.py:219
  452.7 379.9 %reduce-scatter.20.cloned.1.call-start = ((), (), s32[]{:S(2)}) async-start(), calls=%async_computation.14 | async-start | bytes 2211840
  541.5 9.5 %copy-start.35 = (f32[2,96]{1,0:T(2,128)S(1)}, f32[2,96]{1,0:T(2,128)}, u32[]{:S(2)}) copy-start(f32[2,96]{1,0:T(2,128)} %param.56) | copy-start | bytes 2308
  541.5 14.9 %copy-start.37 = (f32[2,24]{1,0:T(2,128)S(1)}, f32[2,24]{1,0:T(2,128)}, u32[]{:S(2)}) copy-start(f32[2,24]{1,0:T(2,128)} %param.50) | copy-start | bytes 580
  544.7 15.9 %copy-start.42 = (f32[768]{0:T(1024)S(1)}, f32[768]{0:T(1024)}, u32[]{:S(2)}) copy-start(f32[768]{0:T(1024)} %get-tuple-element.472) | copy-start | bytes 9220
  544.7 37.5 %copy-start.48 = (f32[2,24]{1,0:T(2,128)S(1)}, f32[2,24]{1,0:T(2,128)}, u32[]{:S(2)}) copy-start(f32[2,24]{1,0:T(2,128)} %param.52) | copy-start | bytes 580
  544.7 37.5 %copy-start.49 = (f32[2,24]{1,0:T(2,128)S(1)}, f32[2,24]{1,0:T(2,128)}, u32[]{:S(2)}) copy-start(f32[2,24]{1,0:T(2,128)} %param.51) | copy-start | bytes 580
  547.5 295.6 %all-reduce.15.cloned.1.call-start = ((), (), s32[]{:S(2)}) async-start(), calls=%async_computation.11 | async-start | bytes 6291456 | tf_op jit(solution)/shard_map/psum | solution.py:211
  582.9 7.4 copy-start.38
  583.5 9.0 copy-start.50
  583.5 9.0 copy-start.51
  583.5 12.4 %copy-start.45 = (f32[4,96]{1,0:T(4,128)S(1)}, f32[4,96]{1,0:T(4,128)}, u32[]{:S(2)}) copy-start(f32[4,96]{1,0:T(4,128)} %param.61) | copy-start | bytes 4612
  583.5 12.4 %copy-start.46 = (f32[4,96]{1,0:T(4,128)S(1)}, f32[4,96]{1,0:T(4,128)}, u32[]{:S(2)}) copy-start(f32[4,96]{1,0:T(4,128)} %param.60) | copy-start | bytes 4612
  583.5 36.4 %copy-start.19 = (f32[192,96]{1,0:T(8,128)S(1)}, f32[192,96]{1,0:T(8,128)}, u32[]{:S(2)}) copy-start(f32[192,96]{1,0:T(8,128)} %param.41) | copy-start | bytes 221188
  583.5 36.4 %copy-start.27 = (f32[192,96]{1,0:T(8,128)S(1)}, f32[192,96]{1,0:T(8,128)}, u32[]{:S(2)}) copy-start(f32[192,96]{1,0:T(8,128)} %param.43) | copy-start | bytes 221188
  583.5 36.4 %copy-start.28 = (f32[192,96]{1,0:T(8,128)S(1)}, f32[192,96]{1,0:T(8,128)}, u32[]{:S(2)}) copy-start(f32[192,96]{1,0:T(8,128)} %param.42) | copy-start | bytes 221188
  583.5 107.5 %copy-start.12 = (f32[96,768]{1,0:T(8,128)S(1)}, f32[96,768]{1,0:T(8,128)}, u32[]{:S(2)}) copy-start(f32[96,768]{1,0:T(8,128)} %param.44) | copy-start | bytes 884740
  583.6 107.5 %copy-start.22 = (f32[96,768]{1,0:T(8,128)S(1)}, f32[96,768]{1,0:T(8,128)}, u32[]{:S(2)}) copy-start(f32[96,768]{1,0:T(8,128)} %param.46) | copy-start | bytes 884740
  583.6 107.5 %copy-start.23 = (f32[96,768]{1,0:T(8,128)S(1)}, f32[96,768]{1,0:T(8,128)}, u32[]{:S(2)}) copy-start(f32[96,768]{1,0:T(8,128)} %param.45) | copy-start | bytes 884740
  583.6 179.5 %copy-start.11 = (f32[768,96]{0,1:T(8,128)S(1)}, f32[768,96]{0,1:T(8,128)}, u32[]{:S(2)}) copy-start(f32[768,96]{0,1:T(8,128)} %param.47) | copy-start | bytes 884740
  583.6 179.5 %copy-start.24 = (f32[768,96]{0,1:T(8,128)S(1)}, f32[768,96]{0,1:T(8,128)}, u32[]{:S(2)}) copy-start(f32[768,96]{0,1:T(8,128)} %param.49) | copy-start | bytes 884740
  621.2 278.9 %copy-start.20 = (f32[192,96]{1,0:T(8,128)}, f32[192,96]{1,0:T(8,128)S(1)}, u32[]{:S(2)}) copy-start(f32[192,96]{1,0:T(8,128)S(1)} %get-tuple-element.444) | copy-start | bytes 221188
  692.8 206.5 %copy-start.14 = (f32[96,768]{1,0:T(8,128)}, f32[96,768]{1,0:T(8,128)S(1)}, u32[]{:S(2)}) copy-start(f32[96,768]{1,0:T(8,128)S(1)} %get-tuple-element.442) | copy-start | bytes 884740
  692.8 206.5 %copy-start.15 = (f32[96,768]{1,0:T(8,128)}, f32[96,768]{1,0:T(8,128)S(1)}, u32[]{:S(2)}) copy-start(f32[96,768]{1,0:T(8,128)S(1)} %get-tuple-element.443) | copy-start | bytes 884740
  843.1 47.6 %copy-start.41 = (f32[2,96]{1,0:T(2,128)S(1)}, f32[2,96]{1,0:T(2,128)}, u32[]{:S(2)}) copy-start(f32[2,96]{1,0:T(2,128)} %copy-done.40) | copy-start | bytes 2308
  843.1 48.2 %copy-start.39 = (f32[2,24]{1,0:T(2,128)S(1)}, f32[2,24]{1,0:T(2,128)}, u32[]{:S(2)}) copy-start(f32[2,24]{1,0:T(2,128)} %copy-done.38) | copy-start | bytes 580
  843.1 55.3 %copy-start.16 = (f32[768,96]{0,1:T(8,128)S(1)}, f32[768,96]{0,1:T(8,128)}, u32[]{:S(2)}) copy-start(f32[768,96]{0,1:T(8,128)} %get-tuple-element.440) | copy-start | bytes 884740
  843.1 55.3 %copy-start.17 = (f32[768,96]{0,1:T(8,128)S(1)}, f32[768,96]{0,1:T(8,128)}, u32[]{:S(2)}) copy-start(f32[768,96]{0,1:T(8,128)} %get-tuple-element.441) | copy-start | bytes 884740
  843.1 57.0 %copy-start.21 = (f32[192,96]{1,0:T(8,128)S(1)}, f32[192,96]{1,0:T(8,128)}, u32[]{:S(2)}) copy-start(f32[192,96]{1,0:T(8,128)} %get-tuple-element.445) | copy-start | bytes 221188
  (25 other events, 98.5 us)
Sparse Core Ops, SparseCore 0:
  143.6 65.7 all-reduce.8
  242.1 68.5 all-reduce.10
  340.1 68.5 all-reduce.12
  590.4 65.0 all-reduce.14
Sparse Core Ops, SparseCore 1:
  146.7 38.5 all-gather.5
  187.9 40.1 all-gather.7
  428.2 61.6 reduce-scatter.23
  493.2 60.6 reduce-scatter.25
  557.2 61.6 reduce-scatter.21
  622.8 68.2 reduce-scatter.15
  694.8 68.2 reduce-scatter.17
  766.8 65.8 reduce-scatter.19
where the time goes:
time: 916 us; the launch traced here: 908 us
  waiting for transfers between devices  356 us (39%)
  blocking collectives  202 us (22%)
  matrix products  136 us (15%)
  local copies, waits for them, and re-layouts  98.7 us (11%)
  other arithmetic  85.6 us (9%)
  between operations  28.7 us (3%)
    unnamed x16, waiting for transfers between devices  80 us
    reduce_scatter x1, waiting for transfers between devices, on_device(): lax.psum_scatter(down_grad, 'dp', scatter_dimension=1, tiled=True)  70.3 us
    reduce_scatter x1, waiting for transfers between devices, on_device(): lax.psum_scatter(up_grad, 'dp', scatter_dimension=0, tiled=True)  69.8 us
    psum x1, waiting for transfers between devices, on_device(): lax.psum(ffn_part.astype(jnp.bfloat16), 'tensor').astype(jnp.float32)  68.4 us
    psum x1, waiting for transfers between devices, on_device(): lax.psum(normed_part.astype(jnp.bfloat16), 'tensor').astype(jnp.float32)  66.1 us
    psum x1, blocking collectives, on_device(): lax.psum(jnp.stack([jnp.stack(weight_sq), jnp.stack(update_sq)]), ('dp',...  39.4 us
    unnamed x2, blocking collectives  39.3 us
    all_gather x1, blocking collectives, on_device(): lax.all_gather(attn_weight.astype(bfloat), 'dp', axis=1, tiled=True)  38.6 us
  transfers between devices with their start and end apart: 12, of which 7 were waited for; matrix products, arithmetic and copies ran while one was open for 22% of the time, Pallas kernels for 0%

commit v1 on v0

--- a/solution.py
+++ b/solution.py
@@ -161,7 +161,9 @@
     ffn_part = jnp.dot(active_low, down_low, preferred_element_type=single)
     summed_two = (
         normed
-        + lax.psum(ffn_part.astype(jnp.bfloat16), "tensor").astype(jnp.float32)
+        + jnp.sum(lax.all_gather(ffn_part.astype(jnp.bfloat16), "tensor"), axis=0).astype(
+            jnp.float32
+        )
         + shift_float[2]
     )
     normal_two, scaled_two = layer_norm(summed_two)

time: 916 us -> 939 us (1.025)
  waiting for transfers between devices: 356 us -> 369 us
    all_gather x0 -> x1, waiting for transfers between devices: none -> 81.9 us  [on_device(): lax.all_gather(ffn_part.astype(jnp.bfloat16), 'tensor')]
    psum x1 -> x0, waiting for transfers between devices: 68.4 us -> none  [on_device(): lax.psum(ffn_part.astype(jnp.bfloat16), 'tensor').astype(jnp.float32)]
where the time goes in v1:
time: 939 us; the launch traced here: 931 us
  waiting for transfers between devices  369 us (39%)
  blocking collectives  202 us (22%)
  matrix products  136 us (14%)
  local copies, waits for them, and re-layouts  98.8 us (11%)
  other arithmetic  94.6 us (10%)
  between operations  28.9 us (3%)
    all_gather x1, waiting for transfers between devices, on_device(): lax.all_gather(ffn_part.astype(jnp.bfloat16), 'tensor')  81.9 us
    unnamed x16, waiting for transfers between devices  80.3 us
    reduce_scatter x1, waiting for transfers between devices, on_device(): lax.psum_scatter(down_grad, 'dp', scatter_dimension=1, tiled=True)  70.2 us
    reduce_scatter x1, waiting for transfers between devices, on_device(): lax.psum_scatter(up_grad, 'dp', scatter_dimension=0, tiled=True)  69.9 us
    psum x1, waiting for transfers between devices, on_device(): lax.psum(normed_part.astype(jnp.bfloat16), 'tensor').astype(jnp.float32)  65.8 us
    psum x1, blocking collectives, on_device(): lax.psum(jnp.stack([jnp.stack(weight_sq), jnp.stack(update_sq)]), ('dp',...  39.6 us
    unnamed x2, blocking collectives  39.5 us
    all_gather x1, blocking collectives, on_device(): lax.all_gather(attn_weight.astype(bfloat), 'dp', axis=1, tiled=True)  38.6 us
  transfers between devices with their start and end apart: 12, of which 7 were waited for; matrix products, arithmetic and copies ran while one was open for 22% of the time, Pallas kernels for 0%

profile of v1, /device:TPU:0, one launch (start us, length us, event | category | flops | bytes accessed | tf_op | source)
XLA Modules:
  0.0 931.4 jit_solution(7307916853402491533)
XLA Ops:
  9.2 38.6 %all_gather.30 = bf16[3,768,192]{2,0,1:T(4,128)(2,1)S(1)} all-gather(bf16[3,96,192]{2,0,1:T(4,128)(2,1)S(1)} %copy.160), channel_id=1, replica_groups=mesh['dp'=8,'tensor'=4] {'dp'}, dimensions={1}, use_global_device_ids=true | all-gather | bytes 995328 | tf_op jit(solution)/shard_map/all_gather | solution.py:129
  47.8 5.2 convolution_bitcast_fusion
  58.8 18.9 %all-gather.1 = bf16[8,24,2]{1,2,0:T(2,128)(2,1)S(1)} all-gather(bf16[1,24,2]{1,2,0:T(2,128)(2,1)S(1)} %convert_bitcast_fusion.2), channel_id=1, replica_groups=mesh['dp'=8,'tensor'=4] {'dp'}, dimensions={0}, use_global_device_ids=true | all-gather | bytes 864 | tf_op jit(solution)/shard_map/all_gather | solution.py:133
  81.7 2.9 fusion.72
  85.5 15.5 %while.26 = (s32[]{:T(128)}, bf16[4,512,3,64]{1,3,2,0:T(8,128)(2,1)}, f32[4,3,512,1]{2,1,3,0:T(4,128)}, bf16[4,512,3,64]{1,3,2,0:T(8,128)(2,1)S(1)}, pred[4,512,...) while((s32[]{:T(128)}, ...), condition=%wide.region_4.5_spmd, body=%wide.region_1.4_spmd.sunk | while | flops 210860544 | bytes 11592281 | solution.py:149
  108.5 31.2 %all_gather.32 = bf16[192,768]{0,1:T(8,128)(2,1)S(1)} all-gather(bf16[192,96]{0,1:T(8,128)(2,1)} %copy.167), channel_id=1, replica_groups=mesh['dp'=8,'tensor'=4] {'dp'}, dimensions={1}, use_global_device_ids=true | all-gather | bytes 331776 | tf_op jit(solution)/shard_map/all_gather | solution.py:130
  139.6 3.9 convolution_convert_fusion.2
  147.1 16.5 %all-gather.2 = bf16[8,96,4]{1,2,0:T(4,128)(2,1)S(1)} all-gather(bf16[1,96,4]{1,2,0:T(4,128)(2,1)S(1)} %convert_bitcast_fusion), channel_id=1, replica_groups=mesh['dp'=8,'tensor'=4] {'dp'}, dimensions={0}, use_global_device_ids=true | all-gather | bytes 6912 | tf_op jit(solution)/shard_map/all_gather | solution.py:136
  166.4 18.0 %all-gather.3 = bf16[8,96,2]{1,2,0:T(2,128)(2,1)S(1)} all-gather(bf16[1,96,2]{1,2,0:T(2,128)(2,1)S(1)} %convert_bitcast_fusion.1), channel_id=1, replica_groups=mesh['dp'=8,'tensor'=4] {'dp'}, dimensions={0}, use_global_device_ids=true | all-gather | bytes 3456 | tf_op jit(solution)/shard_map/all_gather | solution.py:135
  190.0 17.7 %all-reduce = bf16[768]{0:T(1024)(128)(2,1)S(1)} all-reduce(bf16[768]{0:T(1024)(128)(2,1)S(1)} %dynamic-update-slice), channel_id=1, replica_groups=mesh['dp'=8,'tensor'=4] {'dp'}, use_global_device_ids=true, to_apply=%add | all-reduce | flops 768 | bytes 3072
  209.4 3.1 fusion.68
  214.9 20.6 %multiply_convert_fusion.1 = (bf16[2048,768]{1,0:T(8,128)(2,1)}, f32[2048,768]{1,0:T(8,128)}, f32[2048,768]{1,0:T(8,128)}) fusion(f32[768]{0:T(1024)} %convert_element_type.167, bf16[768,768]{1,0:T(8,128)(2,1)} %all-gather.8.cloned.1.call-done, f32[768]{0:T(1024)} %get-tuple-element.367, f32[768]{0:T(1024)S(1)} %get-tuple-element.370, ...), kind=kOutput, calls=%fused_computation.83 | convolution fusion | flops 2533883904 | bytes 23228416 | tf_op jit(solution)/shard_map/dot_general | solution.py:158
  235.5 6.5 convolution_convert_fusion.1
  242.6 81.9 %all-gather.12.cloned.1.call-done = bf16[8192,768]{1,0:T(8,128)(2,1)} async-done(((bf16[2048,768]{1,0:T(8,128)(2,1)}), bf16[8192,768]{1,0:T(8,128)(2,1)}) %all-gather.12.cloned.1.call-update) | async-done | bytes 12582928 | tf_op jit(solution)/shard_map/all_gather | solution.py:164
  324.4 9.0 reduce_sum.465
  333.4 4.8 fusion.119
  340.1 3.6 fusion.61
  343.8 3.8 fusion.58
  347.6 9.4 %convert_reduce_fusion.1 = (f32[768]{0:T(1024)}, bf16[2048,768]{1,0:T(8,128)(2,1)S(1)}) fusion(f32[2048,768]{1,0:T(8,128)S(1)} %bitcast.252, bf16[768,768]{0,1:T(8,128)(2,1)S(1)} %copy-done.57, f32[2048,768]{1,0:T(8,128)S(1)} %get-tuple-element.457, f32[2048,768]{1,0:T(8,128)} %get-tuple-element.471, f32[768]{0:T(1024)S(1)} %copy-done.43), kind=kOutput, calls=%fused_computation.74 | convolution fusion | flops 2444229888 | bytes 23205888 | tf_op jit(solution)/shard_map/td,fd->tf/dot_general | solution.py:178
  358.7 4.0 convolution_convert_fusion
  365.5 65.8 %all-reduce.10.cloned.1.call-done = bf16[2048,768]{1,0:T(8,128)(2,1)} async-done(((bf16[2048,768]{1,0:T(8,128)(2,1)}), bf16[2048,768]{1,0:T(8,128)(2,1)}) %all-reduce.10.cloned.1.call-update) | async-done | bytes 3145744 | tf_op jit(solution)/shard_map/psum | solution.py:183
  431.3 7.3 multiply_reduce_fusion.1
  438.7 8.1 fusion.111
  453.9 5.3 fusion.86
  459.3 7.6 fusion.91
  467.0 7.9 fusion.77
  475.0 4.9 convolution_convert_fusion.3
  479.9 3.2 reshape.246
  488.2 51.0 %while.27 = (s32[]{:T(128)}, bf16[4,512,3,64]{1,3,2,0:T(8,128)(2,1)}, bf16[4,512,3,64]{1,3,2,0:T(8,128)(2,1)}, bf16[4,512,3,64]{1,3,2,0:T(8,128)(2,1)}, bf16[4,5...) while((s32[]{:T(128)}, ...), condition=%wide.region_18.19_spmd, body=%wide.region_16.18_spmd.sunk | while | flops 510884352 | bytes 26381428 | solution.py:195
  539.2 2.6 copy.172
  541.8 2.8 stack_reshape.9
  547.2 2.8 stack_reshape.10
  550.0 2.7 copy.174
  552.7 2.8 stack_reshape.11
  560.5 3.2 fusion.83
  563.7 3.2 copy.187
  567.0 2.8 reshape.265
  582.8 21.8 %all-reduce.3 = (f32[2,192]{1,0:T(2,128)S(1)}, f32[768]{0:T(1024)S(1)}) all-reduce(f32[2,192]{1,0:T(2,128)S(1)} %pad_maximum_fusion.2, f32[768]{0:T(1024)S(1)} %copy-done.42), channel_id=7, replica_groups=mesh['dp'=8,'tensor'=4] {'dp'}, use_global_device_ids=true, to_apply=%region_47.48.clone | all-reduce | flops 1152 | bytes 9216
  606.0 6.7 bitcast_convert_fusion
  622.2 19.2 %reduce-scatter.22.cloned.1.call-done = f32[96,192]{1,0:T(8,128)} async-done(((f32[768,192]{1,0:T(8,128)}), f32[96,192]{1,0:T(8,128)}) %reduce-scatter.22.cloned.1.call-update) | async-done | bytes 73744
  643.7 69.9 %reduce-scatter.16.cloned.1.call-done = f32[96,768]{1,0:T(8,128)} async-done(((f32[768,768]{1,0:T(8,128)}), f32[96,768]{1,0:T(8,128)}) %reduce-scatter.16.cloned.1.call-update) | async-done | bytes 294928 | tf_op jit(solution)/shard_map/reduce_scatter | solution.py:220
  715.5 70.2 %reduce-scatter.18.cloned.1.call-done = f32[768,96]{0,1:T(8,128)} async-done(((f32[768,768]{0,1:T(8,128)}), f32[768,96]{0,1:T(8,128)}) %reduce-scatter.18.cloned.1.call-update) | async-done | bytes 294928 | tf_op jit(solution)/shard_map/reduce_scatter | solution.py:221
  785.6 2.7 multiply_reduce_fusion.8
  788.3 6.3 stack.157
  794.6 60.8 %reduce-scatter.20.cloned.1.call-done = f32[96,576]{1,0:T(8,128)} async-done(((f32[768,576]{1,0:T(8,128)}), f32[96,576]{1,0:T(8,128)}) %reduce-scatter.20.cloned.1.call-update) | async-done | bytes 221200
  859.2 5.9 stack.185
  865.9 6.1 add_convert_fusion
  872.0 39.6 %psum.31 = f32[2,15]{1,0:T(2,128)S(1)} all-reduce(f32[2,15]{1,0:T(2,128)S(1)} %pad_maximum_fusion.3), channel_id=1, replica_groups=mesh['dp'=8,'tensor'=4] {'dp','tensor'}, use_global_device_ids=true, to_apply=%region_67.68 | all-reduce | flops 30 | bytes 240 | tf_op jit(solution)/shard_map/psum | solution.py:273
  (316 shorter events, 160.5 us)
Async XLA Ops:
  8.0 201.4 %all-reduce.8.cloned.1.call-start = ((), (), s32[]{:S(2)}) async-start(), calls=%async_computation.6 | async-start | bytes 6291456 | tf_op jit(solution)/shard_map/psum | solution.py:153
  53.4 27.1 %copy-start.29 = (s32[4,512]{1,0:T(4,128)S(1)}, s32[4,512]{1,0:T(4,128)}, u32[]{:S(2)}) copy-start(s32[4,512]{1,0:T(4,128)} %param.37) | copy-start | bytes 24580
  53.4 27.1 %copy-start.44 = (s32[4,64]{1,0:T(4,128)S(1)}, s32[4,64]{1,0:T(4,128)}, u32[]{:S(2)}) copy-start(s32[4,64]{1,0:T(4,128)} %param.36) | copy-start | bytes 3076
  53.4 27.3 %copy-start.55 = (s32[4]{0:T(128)S(1)}, s32[4]{0:T(128)}, u32[]{:S(2)}) copy-start(s32[4]{0:T(128)} %param.35) | copy-start | bytes 52
  85.5 22.2 %copy-start.18 = (f32[192,96]{1,0:T(8,128)S(1)}, f32[192,96]{1,0:T(8,128)}, u32[]{:S(2)}) copy-start(f32[192,96]{1,0:T(8,128)} %param.41) | copy-start | bytes 221188
  104.8 42.3 %copy-start.31 = (f32[4,96]{1,0:T(4,128)S(1)}, f32[4,96]{1,0:T(4,128)}, u32[]{:S(2)}) copy-start(f32[4,96]{1,0:T(4,128)} %param.59) | copy-start | bytes 4612
  104.8 104.7 %copy-start = (bf16[2048,768]{1,0:T(8,128)(2,1)S(1)}, bf16[2048,768]{1,0:T(8,128)(2,1)}, u32[]{:S(2)}) copy-start(bf16[2048,768]{1,0:T(8,128)(2,1)} %param.33) | copy-start | bytes 9437188
  143.5 71.4 %all-gather.8.cloned.1.call-start = ((), (), s32[]{:S(2)}) async-start(), calls=%async_computation.7 | async-start | bytes 1327104 | tf_op jit(solution)/shard_map/all_gather | solution.py:131
  145.2 90.3 %all-gather.10.cloned.1.call-start = ((), (), s32[]{:S(2)}) async-start(), calls=%async_computation.8 | async-start | bytes 1327104 | tf_op jit(solution)/shard_map/all_gather | solution.py:132
  147.0 177.4 %all-gather.12.cloned.1.call-start = ((), (), s32[]{:S(2)}) async-start(), calls=%async_computation.13 | async-start | bytes 15728640 | tf_op jit(solution)/shard_map/all_gather | solution.py:164
  242.1 189.2 %all-reduce.10.cloned.1.call-start = ((), (), s32[]{:S(2)}) async-start(), calls=%async_computation.9 | async-start | bytes 6291456 | tf_op jit(solution)/shard_map/psum | solution.py:183
  340.1 7.5 slice-start
  347.6 9.4 %copy-start.3 = (f32[2048,768]{1,0:T(8,128)}, f32[2048,768]{1,0:T(8,128)S(1)}, u32[]{:S(2)}) copy-start(f32[2048,768]{1,0:T(8,128)S(1)} %get-tuple-element.457) | copy-start | bytes 18874372
  347.6 11.1 %copy-start.56 = (bf16[768,768]{1,0:T(8,128)(2,1)S(1)}, bf16[768,768]{1,0:T(8,128)(2,1)}, u32[]{:S(2)}) copy-start(bf16[768,768]{1,0:T(8,128)(2,1)} %all-gather.8.cloned.1.call-done) | copy-start | bytes 3538948
  362.7 251.4 %reduce-scatter.24.cloned.1.call-start = ((), (), s32[]{:S(2)}) async-start(), calls=%async_computation.16 | async-start | bytes 442368
  438.6 9.9 %copy-start.34 = (f32[1,768]{1,0:T(1,128)S(1)}, f32[1,768]{1,0:T(1,128)}, u32[]{:S(2)}) copy-start(f32[1,768]{1,0:T(1,128)} %stack.172) | copy-start | bytes 9220
  450.8 166.7 %reduce-scatter.26.cloned.1.call-start = ((), (), s32[]{:S(2)}) async-start(), calls=%async_computation.17 | async-start | bytes 442368
  453.9 187.6 %reduce-scatter.22.cloned.1.call-start = ((), (), s32[]{:S(2)}) async-start(), calls=%async_computation.15 | async-start | bytes 884736
  459.3 254.4 %reduce-scatter.16.cloned.1.call-start = ((), (), s32[]{:S(2)}) async-start(), calls=%async_computation.11 | async-start | bytes 2654208 | tf_op jit(solution)/shard_map/reduce_scatter | solution.py:220
  467.0 318.7 %reduce-scatter.18.cloned.1.call-start = ((), (), s32[]{:S(2)}) async-start(), calls=%async_computation.12 | async-start | bytes 2654208 | tf_op jit(solution)/shard_map/reduce_scatter | solution.py:221
  474.9 380.5 %reduce-scatter.20.cloned.1.call-start = ((), (), s32[]{:S(2)}) async-start(), calls=%async_computation.14 | async-start | bytes 2211840
  563.7 9.5 %copy-start.35 = (f32[2,96]{1,0:T(2,128)S(1)}, f32[2,96]{1,0:T(2,128)}, u32[]{:S(2)}) copy-start(f32[2,96]{1,0:T(2,128)} %param.56) | copy-start | bytes 2308
  563.7 14.9 %copy-start.37 = (f32[2,24]{1,0:T(2,128)S(1)}, f32[2,24]{1,0:T(2,128)}, u32[]{:S(2)}) copy-start(f32[2,24]{1,0:T(2,128)} %param.50) | copy-start | bytes 580
  566.9 15.9 %copy-start.42 = (f32[768]{0:T(1024)S(1)}, f32[768]{0:T(1024)}, u32[]{:S(2)}) copy-start(f32[768]{0:T(1024)} %get-tuple-element.472) | copy-start | bytes 9220
  567.0 37.7 %copy-start.48 = (f32[2,24]{1,0:T(2,128)S(1)}, f32[2,24]{1,0:T(2,128)}, u32[]{:S(2)}) copy-start(f32[2,24]{1,0:T(2,128)} %param.52) | copy-start | bytes 580
  567.0 37.7 %copy-start.49 = (f32[2,24]{1,0:T(2,128)S(1)}, f32[2,24]{1,0:T(2,128)}, u32[]{:S(2)}) copy-start(f32[2,24]{1,0:T(2,128)} %param.51) | copy-start | bytes 580
  569.8 296.1 %all-reduce.12.cloned.1.call-start = ((), (), s32[]{:S(2)}) async-start(), calls=%async_computation.10 | async-start | bytes 6291456 | tf_op jit(solution)/shard_map/psum | solution.py:213
  605.3 7.4 copy-start.38
  605.9 9.0 copy-start.50
  605.9 9.0 copy-start.51
  605.9 12.4 %copy-start.45 = (f32[4,96]{1,0:T(4,128)S(1)}, f32[4,96]{1,0:T(4,128)}, u32[]{:S(2)}) copy-start(f32[4,96]{1,0:T(4,128)} %param.61) | copy-start | bytes 4612
  605.9 12.4 %copy-start.46 = (f32[4,96]{1,0:T(4,128)S(1)}, f32[4,96]{1,0:T(4,128)}, u32[]{:S(2)}) copy-start(f32[4,96]{1,0:T(4,128)} %param.60) | copy-start | bytes 4612
  606.0 36.5 %copy-start.19 = (f32[192,96]{1,0:T(8,128)S(1)}, f32[192,96]{1,0:T(8,128)}, u32[]{:S(2)}) copy-start(f32[192,96]{1,0:T(8,128)} %param.41) | copy-start | bytes 221188
  606.0 36.5 %copy-start.27 = (f32[192,96]{1,0:T(8,128)S(1)}, f32[192,96]{1,0:T(8,128)}, u32[]{:S(2)}) copy-start(f32[192,96]{1,0:T(8,128)} %param.43) | copy-start | bytes 221188
  606.0 36.5 %copy-start.28 = (f32[192,96]{1,0:T(8,128)S(1)}, f32[192,96]{1,0:T(8,128)}, u32[]{:S(2)}) copy-start(f32[192,96]{1,0:T(8,128)} %param.42) | copy-start | bytes 221188
  606.0 107.7 %copy-start.12 = (f32[96,768]{1,0:T(8,128)S(1)}, f32[96,768]{1,0:T(8,128)}, u32[]{:S(2)}) copy-start(f32[96,768]{1,0:T(8,128)} %param.44) | copy-start | bytes 884740
  606.0 107.7 %copy-start.22 = (f32[96,768]{1,0:T(8,128)S(1)}, f32[96,768]{1,0:T(8,128)}, u32[]{:S(2)}) copy-start(f32[96,768]{1,0:T(8,128)} %param.46) | copy-start | bytes 884740
  606.0 107.7 %copy-start.23 = (f32[96,768]{1,0:T(8,128)S(1)}, f32[96,768]{1,0:T(8,128)}, u32[]{:S(2)}) copy-start(f32[96,768]{1,0:T(8,128)} %param.45) | copy-start | bytes 884740
  606.0 179.6 %copy-start.11 = (f32[768,96]{0,1:T(8,128)S(1)}, f32[768,96]{0,1:T(8,128)}, u32[]{:S(2)}) copy-start(f32[768,96]{0,1:T(8,128)} %param.47) | copy-start | bytes 884740
  606.0 179.6 %copy-start.24 = (f32[768,96]{0,1:T(8,128)S(1)}, f32[768,96]{0,1:T(8,128)}, u32[]{:S(2)}) copy-start(f32[768,96]{0,1:T(8,128)} %param.49) | copy-start | bytes 884740
  643.7 279.4 %copy-start.20 = (f32[192,96]{1,0:T(8,128)}, f32[192,96]{1,0:T(8,128)S(1)}, u32[]{:S(2)}) copy-start(f32[192,96]{1,0:T(8,128)S(1)} %get-tuple-element.444) | copy-start | bytes 221188
  715.5 206.8 %copy-start.14 = (f32[96,768]{1,0:T(8,128)}, f32[96,768]{1,0:T(8,128)S(1)}, u32[]{:S(2)}) copy-start(f32[96,768]{1,0:T(8,128)S(1)} %get-tuple-element.442) | copy-start | bytes 884740
  715.5 206.8 %copy-start.15 = (f32[96,768]{1,0:T(8,128)}, f32[96,768]{1,0:T(8,128)S(1)}, u32[]{:S(2)}) copy-start(f32[96,768]{1,0:T(8,128)S(1)} %get-tuple-element.443) | copy-start | bytes 884740
  865.8 47.8 %copy-start.41 = (f32[2,96]{1,0:T(2,128)S(1)}, f32[2,96]{1,0:T(2,128)}, u32[]{:S(2)}) copy-start(f32[2,96]{1,0:T(2,128)} %copy-done.40) | copy-start | bytes 2308
  865.8 48.4 %copy-start.39 = (f32[2,24]{1,0:T(2,128)S(1)}, f32[2,24]{1,0:T(2,128)}, u32[]{:S(2)}) copy-start(f32[2,24]{1,0:T(2,128)} %copy-done.38) | copy-start | bytes 580
  865.8 55.5 %copy-start.16 = (f32[768,96]{0,1:T(8,128)S(1)}, f32[768,96]{0,1:T(8,128)}, u32[]{:S(2)}) copy-start(f32[768,96]{0,1:T(8,128)} %get-tuple-element.440) | copy-start | bytes 884740
  865.9 55.5 %copy-start.17 = (f32[768,96]{0,1:T(8,128)S(1)}, f32[768,96]{0,1:T(8,128)}, u32[]{:S(2)}) copy-start(f32[768,96]{0,1:T(8,128)} %get-tuple-element.441) | copy-start | bytes 884740
  865.9 57.2 %copy-start.21 = (f32[192,96]{1,0:T(8,128)S(1)}, f32[192,96]{1,0:T(8,128)}, u32[]{:S(2)}) copy-start(f32[192,96]{1,0:T(8,128)} %get-tuple-element.445) | copy-start | bytes 221188
  (25 other events, 98.7 us)
Sparse Core Ops, SparseCore 0:
  143.6 65.7 all-reduce.7
  242.2 82.2 all-gather.11
  362.8 68.4 all-reduce.9
  612.9 64.8 all-reduce.11
Sparse Core Ops, SparseCore 1:
  146.8 38.7 all-gather.7
  188.1 40.2 all-gather.9
  450.8 61.6 reduce-scatter.23
  515.8 60.5 reduce-scatter.25
  579.7 61.7 reduce-scatter.21
  645.3 68.3 reduce-scatter.15
  717.4 68.2 reduce-scatter.17
  789.4 66.0 reduce-scatter.19
